TPU v7x, 32 devices: a whole 2x2x4 slice. The times are simulated.
32 devices in a mesh: px: 4 (over x, core), py: 8 (over z, y).
Axes of the slice: x: 2, y: 2, z: 4, core: 2. Of those that a mesh axis runs over, the one named last changes fastest.
Arguments:
- displacement: float32 [6, 64, 1024], P(None, 'px', 'py'), may hold values from -4 to 4
- velocity: float32 [6, 64, 1024], P(None, 'px', 'py'), may hold values from -6 to 6
- load: float32 [6, 64, 1024], P(None, 'px', 'py'), may hold values from -24 to 24
- inv_mass: float32 [6, 64, 1024], P(None, 'px', 'py'), may hold values from 0.2 to 1
- history: float32 [128, 64, 1024], P(None, 'px', 'py'), may hold values from -6 to 6
- contact_home: float32 [128, 64, 1024], P(None, 'px', 'py'), may hold values from 0.25 to 4
- recv_contact: float32 [4, 8, 128, 1216], P('px', 'py'), may hold values from 0.25 to 4
- stiff_base: float32 [24, 24], replicated, as said below
- strain_map: float32 [128, 24], replicated, may hold values from -1.25 to 1.25
- slot_table: int32 [4, 8, 1216], P('px', 'py'), may hold values from 0 to 2048, as said below
Outputs:
- springback: float32 [6, 64, 1024], P(None, 'px', 'py')
- velocity_out: float32 [6, 64, 1024], P(None, 'px', 'py')
- history_out: float32 [128, 64, 1024], P(None, 'px', 'py')
- residual: float32 [6, 64, 1024], P(None, 'px', 'py')
Inputs may be any that keep to these rules, and one draw needn't show every extreme that they name: `slot_table`: for each source block and destination device d, the slots d * 38 .. d * 38 + 37 hold distinct local shell indices first and then 16 * 128; no shell appears twice in one source block; no block sends to itself; every source block fills all 38 slots toward some destination, and about half of the source blocks fill all slots toward every other device. `stiff_base`: Symmetric, with diagonal entries of 5 to 7 and off-diagonal entries of magnitude at most 0.2.
All inputs are finite; a program needn't handle non-finite values.
Results may differ from a plain program's by a relative error of at most 0.0003.
Values sent between devices are 32-bit elements; how exact they have to be, the bound alone decides.
A program may use at most 128 MiB of HBM per device.

v0:
```python
import jax
import jax.numpy as jnp
from jax import lax
from jax.sharding import PartitionSpec as P

ITERS = 2


HIGH = lax.Precision.HIGHEST
STEP = 0.2
CORNERS = ((0, 0), (1, 0), (0, 1), (1, 1))


def with_halo(shard, sides, width):
    for axis, dim in sides:
        devices, length = (lax.axis_size(axis), shard.shape[dim])
        up = [(i, (i + 1) % devices) for i in range(devices - 1)]
        down = [(j, i) for i, j in up]
        last = lax.slice_in_dim(shard, length - width, length, axis=dim)
        leading = lax.slice_in_dim(shard, 0, width, axis=dim)
        before = lax.ppermute(last, axis, up)
        after = lax.ppermute(leading, axis, down)
        shard = jnp.concatenate([before, shard, after], axis=dim)
    return shard


def shifted(shard, axis, by):
    devices = lax.axis_size(axis)
    pairs = [(i, i + by) for i in range(devices) if 0 <= i + by < devices]
    return lax.ppermute(shard, axis, pairs)


def apply_field(field, multiply):
    rows, cols = (field.shape[1], field.shape[2])
    padded = with_halo(field, (("px", 1), ("py", 2)), 1)
    shells = jnp.concatenate(
        [padded[:, dx : dx + rows + 1, dy : dy + cols + 1] for dx, dy in CORNERS], axis=0
    )
    forces = multiply(shells)
    row_keep = (jnp.arange(rows + 1) > 0) | (lax.axis_index("px") > 0)
    col_keep = (jnp.arange(cols + 1) > 0) | (lax.axis_index("py") > 0)
    keep = (row_keep[:, None] & col_keep[None, :]).astype(jnp.float32)
    forces = forces * keep[None, :, :]
    total = jnp.zeros((6, rows, cols), jnp.float32)
    for index, (dx, dy) in enumerate(CORNERS):
        total = (
            total
            + forces[6 * index : 6 * index + 6, 1 - dx : 1 - dx + rows, 1 - dy : 1 - dy + cols]
        )
    return (total, shells)


def global_sum(value):
    return lax.psum(value, ("px", "py"))


def shards(
    displacement,
    velocity,
    load,
    inv_mass,
    history,
    contact_home,
    recv_contact,
    stiff_base,
    strain_map,
    slot_table,
):
    hist = history.shape[0]
    rows, cols = (displacement.shape[1], displacement.shape[2])
    cells = rows * cols

    def with_base(shells):
        return jnp.einsum("ab,bxy->axy", stiff_base, shells, precision=HIGH)

    force_start, start_shells = apply_field(displacement, with_base)
    velocity_out = velocity + STEP * inv_mass * (load - force_start)
    moved = displacement + STEP * velocity_out
    own = start_shells[:, 1:, 1:].reshape(24, cells)
    history_new = history.reshape(hist, cells) + jnp.dot(strain_map, own, precision=HIGH)
    pairs = (strain_map[:, :, None] * strain_map[:, None, :]).reshape(hist, 576)
    targets = slot_table.reshape(-1)
    devices = lax.axis_size("px") * lax.axis_size("py")
    width = targets.shape[0] // devices
    held = recv_contact.reshape(hist, devices, width)
    contact_flat = contact_home.reshape(hist, cells)
    fetched = lax.all_to_all(held, ("px", "py"), split_axis=1, concat_axis=1, tiled=True)
    merged = contact_flat.at[:, targets].set(fetched.reshape(hist, devices * width), mode="drop")
    weights = jax.nn.softplus(history_new) * merged
    tangent = stiff_base.reshape(576, 1) + jnp.dot(pairs.T, weights, precision=HIGH)
    tangent = tangent.reshape(576, rows, cols)
    lower_row = shifted(tangent[:, -1:, :], "px", 1)
    tall = jnp.concatenate([lower_row, tangent], axis=1)
    lower_col = shifted(tall[:, :, -1:], "py", 1)
    extended = jnp.concatenate([lower_col, tall], axis=2).reshape(24, 24, rows + 1, cols + 1)

    def with_tangent(shells):
        return jnp.einsum("abxy,bxy->axy", extended, shells, precision=HIGH)

    rhs = load - force_start
    solution = jnp.zeros_like(rhs)
    residual = rhs
    direction = rhs
    norm_now = global_sum(jnp.sum(residual * residual))
    for step in range(ITERS):
        image = apply_field(direction, with_tangent)[0]
        alpha = norm_now / global_sum(jnp.sum(direction * image))
        solution = solution + alpha * direction
        residual = residual - alpha * image
        if step + 1 < ITERS:
            norm_next = global_sum(jnp.sum(residual * residual))
            direction = residual + norm_next / norm_now * direction
            norm_now = norm_next
    return (moved + solution, velocity_out, history_new.reshape(hist, rows, cols), residual)


def solution(mesh):
    return jax.shard_map(
        shards,
        mesh=mesh,
        in_specs=(
            P(None, "px", "py"),
            P(None, "px", "py"),
            P(None, "px", "py"),
            P(None, "px", "py"),
            P(None, "px", "py"),
            P(None, "px", "py"),
            P("px", "py", None, None),
            P(),
            P(),
            P("px", "py", None),
        ),
        out_specs=(
            P(None, "px", "py"),
            P(None, "px", "py"),
            P(None, "px", "py"),
            P(None, "px", "py"),
        ),
        check_vma=False,
    )
```

profile of v0, /device:TPU:0, one launch (start us, length us, event | category | flops | bytes accessed | tf_op | source)
XLA Modules:
  0.0 257.1 jit_solution(14009452084290173338)
XLA Ops:
  0.6 0.0 copy-start.5
  0.6 0.0 copy-start.9
  0.7 0.8 fusion.41
  1.5 2.3 collective-permute-start
  3.8 1.3 collective-permute-start.1
  5.1 2.0 reshape.113
  7.1 9.3 %all-to-all-start = ((f32[128,32,38]{0,2,1:T(8,128)}), f32[128,32,38]{0,2,1:T(8,128)}, u32[]{:S(2)}, u32[]{:S(2)}) async-start(f32[128,32,38]{0,2,1:T(8,128)} %reshape.113), calls=%async_computation | async-start | bytes 1310720 | tf_op jit(solution)/shard_map/all_to_all | solution.py:87
  16.4 0.8 broadcast_multiply_fusion
  17.3 0.1 and_convert_fusion
  17.3 0.8 copy_dynamic-update-slice_fusion
  18.2 0.1 fusion.38
  18.3 1.3 collective-permute-start.3
  19.6 4.5 %collective-permute-start.2 = (f32[6,18,1]{2,0,1:T(8,128)S(1)}, f32[6,18,1]{2,0,1:T(8,128)S(1)}, u32[]{:S(2)}, u32[]{:S(2)}) collective-permute-start(f32[6,18,1]{2,0,1:T(8,128)S(1)} %get-tuple-element.47), channel_id=1, source_target_pairs={{0,1},{1,2},{2,3},{3,4},{4,5},{5,6},{6,7},{8,9},{9,10},{10,11},{11... | collective-permute-start | bytes 1304 | tf_op jit(solution)/shard_map/ppermute | solution.py:21
  24.1 1.3 fusion.29
  25.4 0.8 add.85
  26.2 1.6 copy.68
  27.8 1.6 copy.66
  29.4 0.1 fusion.25
  29.6 0.6 fusion.1
  30.2 0.1 fusion.26
  30.3 1.3 collective-permute-start.5
  31.6 3.0 %collective-permute-start.4 = (f32[6,1,128]{2,0,1:T(8,128)S(1)}, f32[6,1,128]{2,0,1:T(8,128)S(1)}, u32[]{:S(2)}, u32[]{:S(2)}) collective-permute-start(f32[6,1,128]{2,0,1:T(8,128)S(1)} %get-tuple-element.52), channel_id=1, source_target_pairs={{0,8},{8,16},{16,24},{1,9},{9,17},{17,25},{2,10},{10,18},{18,26},{... | collective-permute-start | bytes 9224 | tf_op jit(solution)/shard_map/ppermute | solution.py:21
  34.7 2.9 %fusion = f32[128,2048]{0,1:T(8,128)S(1)} fusion(f32[128,2048]{0,1:T(8,128)S(1)} %bitcast.56, f32[128,24]{0,1:T(8,128)S(1)} %copy-done.5, f32[6,18,1]{2,0,1:T(8,128)} %copy-done.2, f32[6,18,128]{2,0,1:T(8,128)} %copy-done.1, f32[6,17,129]{2,0,1:T(8,128)S(1)} %get-tuple-element.46, f32[6,17,129]{2,0,1:T(8,128)S(1)} %get-tuple-element.45, ...), kind=kOutput, calls=%fused_computation.7 | convolution fusion | flops 76005376 | bytes 2270864 | tf_op jit(solution)/shard_map/dot_general | solution.py:80
  37.6 0.1 fusion.37
  37.7 4.5 %collective-permute-start.6 = (f32[6,18,1]{2,0,1:T(8,128)S(1)}, f32[6,18,1]{2,0,1:T(8,128)S(1)}, u32[]{:S(2)}, u32[]{:S(2)}) collective-permute-start(f32[6,18,1]{2,0,1:T(8,128)S(1)} %get-tuple-element.43), channel_id=1, source_target_pairs={{0,1},{1,2},{2,3},{3,4},{4,5},{5,6},{6,7},{8,9},{9,10},{10,11},{11... | collective-permute-start | bytes 1304 | tf_op jit(solution)/shard_map/ppermute | solution.py:21
  42.2 1.3 collective-permute-start.7
  43.5 1.1 reshape.119
  44.6 6.6 %scatter_custom_fusion = f32[128,2048]{0,1:T(8,128)S(1)} fusion(f32[128,2048]{0,1:T(8,128)S(1)} %bitcast.55, s32[1216]{0:T(1024)} %fusion.29, f32[128,1216]{0,1:T(8,128)S(1)} %reshape.119), kind=kCustom, calls=%fused_computation.17 | custom fusion | bytes 1671168 | tf_op jit(solution)/shard_map/scatter | solution.py:88
  51.3 6.0 %convolution_add_fusion = f32[576,2048]{1,0:T(8,128)} fusion(f32[128,576]{0,1:T(8,128)S(1)} %bitcast.57, f32[576]{0:T(1024)S(1)} %add.85, f32[128,2048]{0,1:T(8,128)S(1)} %scatter_custom_fusion, f32[128,2048]{0,1:T(8,128)S(1)} %fusion), kind=kOutput, calls=%fused_computation.4 | convolution fusion | flops 1814953984 | bytes 7112960 | tf_op jit(solution)/shard_map/dot_general | solution.py:90
  57.3 5.8 %copy.92 = f32[576,2048]{0,1:T(8,128)} copy(f32[576,2048]{1,0:T(8,128)} %convolution_add_fusion) | data formatting | bytes 9437184 | tf_op jit(solution)/shard_map/reshape | solution.py:91
  63.0 1.1 slice.188
  64.2 2.9 %collective-permute-start.8 = (f32[576,1,128]{0,2,1:T(8,128)S(1)}, f32[576,1,128]{0,2,1:T(8,128)S(1)}, u32[]{:S(2)}, u32[]{:S(2)}) collective-permute-start(f32[576,1,128]{0,2,1:T(8,128)S(1)} %slice.188), channel_id=1, source_target_pairs={{0,8},{8,16},{16,24},{1,9},{9,17},{17,25},{2,10},{10,18},{18,26},{... | collective-permute-start | bytes 884744 | tf_op jit(solution)/shard_map/ppermute | solution.py:30
  67.1 0.1 maximum_maximum_fusion.1
  67.2 1.0 collective-permute-done.8
  68.2 1.0 pad_maximum_fusion.6
  69.3 5.1 %collective-permute-start.9 = (f32[576,17,1]{0,2,1:T(1,128)S(1)}, f32[576,17,1]{0,2,1:T(1,128)S(1)}, u32[]{:S(2)}, u32[]{:S(2)}) collective-permute-start(f32[576,17,1]{0,2,1:T(1,128)S(1)} %pad_maximum_fusion.6), channel_id=1, source_target_pairs={{0,1},{1,2},{2,3},{3,4},{4,5},{5,6},{6,7},{8,9},{9,10},{10,11},{11... | collective-permute-start | bytes 117512 | tf_op jit(solution)/shard_map/ppermute | solution.py:30
  74.4 0.1 maximum_bitcast_fusion
  74.5 1.4 collective-permute-done.9
  75.9 3.0 %maximum_maximum_fusion = f32[576,17,129]{0,2,1:T(8,128)} fusion(f32[576,16,128]{0,2,1:T(8,128)S(1)} %bitcast.53, f32[576,1,128]{0,2,1:T(8,128)S(1)} %collective-permute-done.8, f32[576,17,1]{0,2,1:T(1,128)S(1)} %collective-permute-done.9), kind=kLoop, calls=%fused_computation.3 | loop fusion | flops 2526336 | bytes 10105344 | tf_op jit(solution)/shard_map/concatenate | solution.py:95
  78.9 8.7 %copy.90 = f32[576,17,129]{2,0,1:T(8,128)} copy(f32[576,17,129]{0,2,1:T(8,128)} %maximum_maximum_fusion) | data formatting | bytes 10105344
  87.6 5.9 %multiply_reduce_fusion.1 = f32[17,129,24]{1,2,0:T(8,128)S(1)} fusion(f32[17,129,24,24]{1,2,3,0:T(8,128)} %bitcast.49, f32[17,129,24]{1,2,0:T(8,128)S(1)} %maximum_bitcast_fusion), kind=kLoop, calls=%fused_computation.2 | loop fusion | flops 2473704 | bytes 5473728 | tf_op jit(solution)/shard_map/abxy,bxy->axy/dot_general | solution.py:98
  93.5 0.7 multiply_reduce_fusion.4
  94.2 50.0 %all-reduce = (f32[]{:T(128)}, f32[]{:T(128)}) all-reduce(f32[]{:T(128)} %get-tuple-element.21, f32[]{:T(128)} %get-tuple-element.20), channel_id=1, replica_groups=mesh['px'=4,'py'=8] {'px','py'}, use_global_device_ids=true, to_apply=%region_1.2 | all-reduce | flops 2 | bytes 16 | tf_op jit(solution)/shard_map/psum | solution.py:54
  145.5 0.6 multiply_reduce_fusion.3
  146.1 40.2 %psum.30 = f32[]{:T(128)} all-reduce(f32[]{:T(128)} %multiply_reduce_fusion.3), channel_id=1, replica_groups=mesh['px'=4,'py'=8] {'px','py'}, use_global_device_ids=true, to_apply=%region_6.7 | all-reduce | flops 1 | bytes 8 | tf_op jit(solution)/shard_map/psum | solution.py:54
  187.7 1.3 collective-permute-start.11
  189.0 3.0 %collective-permute-start.10 = (f32[6,1,128]{2,0,1:T(8,128)S(1)}, f32[6,1,128]{2,0,1:T(8,128)S(1)}, u32[]{:S(2)}, u32[]{:S(2)}) collective-permute-start(f32[6,1,128]{2,0,1:T(8,128)S(1)} %get-tuple-element.50), channel_id=1, source_target_pairs={{0,8},{8,16},{16,24},{1,9},{9,17},{17,25},{2,10},{10,18},{18,26},{... | collective-permute-start | bytes 9224 | tf_op jit(solution)/shard_map/ppermute | solution.py:21
  192.1 0.8 collective-permute-done.10
  192.9 0.1 fusion.36
  193.0 4.4 %collective-permute-start.12 = (f32[6,18,1]{2,0,1:T(8,128)S(1)}, f32[6,18,1]{2,0,1:T(8,128)S(1)}, u32[]{:S(2)}, u32[]{:S(2)}) collective-permute-start(f32[6,18,1]{2,0,1:T(8,128)S(1)} %get-tuple-element.39), channel_id=1, source_target_pairs={{0,1},{1,2},{2,3},{3,4},{4,5},{5,6},{6,7},{8,9},{9,10},{10,11},{11... | collective-permute-start | bytes 1304 | tf_op jit(solution)/shard_map/ppermute | solution.py:21
  197.3 1.3 collective-permute-start.13
  198.6 1.4 copy.74
  200.0 4.3 %collective-permute-done.13 = f32[6,18,1]{2,0,1:T(8,128)S(1)} collective-permute-done((f32[6,18,1]{2,0,1:T(8,128)S(1)}, f32[6,18,1]{2,0,1:T(8,128)S(1)}, u32[]{:S(2)}, u32[]{:S(2)}) %collective-permute-start.13) | collective-permute-done | bytes 464 | tf_op jit(solution)/shard_map/ppermute | solution.py:22
  204.3 0.1 maximum_maximum_fusion.2
  204.5 0.1 maximum_bitcast_fusion.1
  204.6 0.0 copy-start.4
  204.6 0.0 copy-start.6
  204.6 5.9 %multiply_reduce_fusion = f32[17,129,24]{1,2,0:T(8,128)S(1)} fusion(f32[17,129,24,24]{1,2,3,0:T(8,128)} %bitcast.50, f32[17,129,24]{1,2,0:T(8,128)S(1)} %maximum_bitcast_fusion.1), kind=kLoop, calls=%fused_computation.1 | loop fusion | flops 2473704 | bytes 5473728 | tf_op jit(solution)/shard_map/abxy,bxy->axy/dot_general | solution.py:98
  210.6 0.7 multiply_reduce_fusion.2
  211.3 42.5 %psum.31 = f32[]{:T(128)} all-reduce(f32[]{:T(128)} %get-tuple-element.26), channel_id=1, replica_groups=mesh['px'=4,'py'=8] {'px','py'}, use_global_device_ids=true, to_apply=%region_8.9 | all-reduce | flops 1 | bytes 8 | tf_op jit(solution)/shard_map/psum | solution.py:54
  255.1 0.1 add_add_fusion
  255.2 0.6 copy.72
  255.9 0.6 copy.73
  256.5 0.6 copy.75
  (43 shorter events, 0.3 us)
Async XLA Ops:
  0.6 34.0 %copy-start.5 = (f32[128,24]{0,1:T(8,128)S(1)}, f32[128,24]{0,1:T(8,128)}, u32[]{:S(2)}) copy-start(f32[128,24]{0,1:T(8,128)} %param.18) | copy-start | bytes 36868
  0.6 28.9 %copy-start.9 = (f32[24,24]{1,0:T(8,128)S(1)}, f32[24,24]{1,0:T(8,128)}, u32[]{:S(2)}) copy-start(f32[24,24]{1,0:T(8,128)} %param.17) | copy-start | bytes 6916
  0.7 29.5 %copy-start.8 = (f32[6,16,128]{2,1,0:T(8,128)S(1)}, f32[6,16,128]{2,1,0:T(8,128)}, u32[]{:S(2)}) copy-start(f32[6,16,128]{2,1,0:T(8,128)} %param.12) | copy-start | bytes 147460
  1.5 15.9 %collective-permute-start = (f32[6,1,128]{2,0,1:T(8,128)S(1)}, f32[6,1,128]{2,0,1:T(8,128)S(1)}, u32[]{:S(2)}, u32[]{:S(2)}) collective-permute-start(f32[6,1,128]{2,0,1:T(8,128)S(1)} %copy.109), channel_id=1, source_target_pairs={{0,8},{8,16},{16,24},{1,9},{9,17},{17,25},{2,10},{10,18},{18,26},{... | collective-permute-start | bytes 9224 | tf_op jit(solution)/shard_map/ppermute | solution.py:21
  3.8 14.3 %collective-permute-start.1 = (f32[6,1,128]{2,0,1:T(8,128)S(1)}, f32[6,1,128]{2,0,1:T(8,128)S(1)}, u32[]{:S(2)}, u32[]{:S(2)}) collective-permute-start(f32[6,1,128]{2,0,1:T(8,128)S(1)} %copy.110), channel_id=1, source_target_pairs={{8,0},{16,8},{24,16},{9,1},{17,9},{25,17},{10,2},{18,10},{26,18},{... | collective-permute-start | bytes 9224 | tf_op jit(solution)/shard_map/ppermute | solution.py:22
  7.1 36.4 %all-to-all-start = ((f32[128,32,38]{0,2,1:T(8,128)}), f32[128,32,38]{0,2,1:T(8,128)}, u32[]{:S(2)}, u32[]{:S(2)}) async-start(f32[128,32,38]{0,2,1:T(8,128)} %reshape.113), calls=%async_computation | async-start | bytes 1310720 | tf_op jit(solution)/shard_map/all_to_all | solution.py:87
  18.2 16.5 %copy-start.1 = (f32[6,18,128]{2,0,1:T(8,128)}, f32[6,18,128]{2,0,1:T(8,128)S(1)}, u32[]{:S(2)}) copy-start(f32[6,18,128]{2,0,1:T(8,128)S(1)} %constant_dynamic-update-slice_fusion) | copy-start | bytes 165892
  18.3 11.1 %collective-permute-start.3 = (f32[6,18,1]{2,0,1:T(8,128)S(1)}, f32[6,18,1]{2,0,1:T(8,128)S(1)}, u32[]{:S(2)}, u32[]{:S(2)}) collective-permute-start(f32[6,18,1]{2,0,1:T(8,128)S(1)} %get-tuple-element.48), channel_id=1, source_target_pairs={{1,0},{2,1},{3,2},{4,3},{5,4},{6,5},{7,6},{9,8},{10,9},{11,10},{12... | collective-permute-start | bytes 1304 | tf_op jit(solution)/shard_map/ppermute | solution.py:22
  19.6 9.9 %collective-permute-start.2 = (f32[6,18,1]{2,0,1:T(8,128)S(1)}, f32[6,18,1]{2,0,1:T(8,128)S(1)}, u32[]{:S(2)}, u32[]{:S(2)}) collective-permute-start(f32[6,18,1]{2,0,1:T(8,128)S(1)} %get-tuple-element.47), channel_id=1, source_target_pairs={{0,1},{1,2},{2,3},{3,4},{4,5},{5,6},{6,7},{8,9},{9,10},{10,11},{11... | collective-permute-start | bytes 1304 | tf_op jit(solution)/shard_map/ppermute | solution.py:21
  29.4 5.2 %copy-start.2 = (f32[6,18,1]{2,0,1:T(8,128)}, f32[6,18,1]{2,0,1:T(8,128)S(1)}, u32[]{:S(2)}) copy-start(f32[6,18,1]{2,0,1:T(8,128)S(1)} %collective-permute-done.3) | copy-start | bytes 1300
  29.4 5.2 %copy-start.3 = (f32[6,18,1]{2,0,1:T(8,128)}, f32[6,18,1]{2,0,1:T(8,128)S(1)}, u32[]{:S(2)}) copy-start(f32[6,18,1]{2,0,1:T(8,128)S(1)} %collective-permute-done.2) | copy-start | bytes 1300
  30.3 7.3 %collective-permute-start.5 = (f32[6,1,128]{2,0,1:T(8,128)S(1)}, f32[6,1,128]{2,0,1:T(8,128)S(1)}, u32[]{:S(2)}, u32[]{:S(2)}) collective-permute-start(f32[6,1,128]{2,0,1:T(8,128)S(1)} %get-tuple-element.53), channel_id=1, source_target_pairs={{8,0},{16,8},{24,16},{9,1},{17,9},{25,17},{10,2},{18,10},{26,18},{... | collective-permute-start | bytes 9224 | tf_op jit(solution)/shard_map/ppermute | solution.py:22
  31.6 6.0 %collective-permute-start.4 = (f32[6,1,128]{2,0,1:T(8,128)S(1)}, f32[6,1,128]{2,0,1:T(8,128)S(1)}, u32[]{:S(2)}, u32[]{:S(2)}) collective-permute-start(f32[6,1,128]{2,0,1:T(8,128)S(1)} %get-tuple-element.52), channel_id=1, source_target_pairs={{0,8},{8,16},{16,24},{1,9},{9,17},{17,25},{2,10},{10,18},{18,26},{... | collective-permute-start | bytes 9224 | tf_op jit(solution)/shard_map/ppermute | solution.py:21
  37.7 29.3 %collective-permute-start.6 = (f32[6,18,1]{2,0,1:T(8,128)S(1)}, f32[6,18,1]{2,0,1:T(8,128)S(1)}, u32[]{:S(2)}, u32[]{:S(2)}) collective-permute-start(f32[6,18,1]{2,0,1:T(8,128)S(1)} %get-tuple-element.43), channel_id=1, source_target_pairs={{0,1},{1,2},{2,3},{3,4},{4,5},{5,6},{6,7},{8,9},{9,10},{10,11},{11... | collective-permute-start | bytes 1304 | tf_op jit(solution)/shard_map/ppermute | solution.py:21
  42.2 24.8 %collective-permute-start.7 = (f32[6,18,1]{2,0,1:T(8,128)S(1)}, f32[6,18,1]{2,0,1:T(8,128)S(1)}, u32[]{:S(2)}, u32[]{:S(2)}) collective-permute-start(f32[6,18,1]{2,0,1:T(8,128)S(1)} %get-tuple-element.44), channel_id=1, source_target_pairs={{1,0},{2,1},{3,2},{4,3},{5,4},{6,5},{7,6},{9,8},{10,9},{11,10},{12... | collective-permute-start | bytes 1304 | tf_op jit(solution)/shard_map/ppermute | solution.py:22
  63.0 12.8 %copy-start = (f32[576,2048]{0,1:T(8,128)S(1)}, f32[576,2048]{0,1:T(8,128)}, u32[]{:S(2)}) copy-start(f32[576,2048]{0,1:T(8,128)} %copy.92) | copy-start | bytes 14155780
  64.2 4.1 %collective-permute-start.8 = (f32[576,1,128]{0,2,1:T(8,128)S(1)}, f32[576,1,128]{0,2,1:T(8,128)S(1)}, u32[]{:S(2)}, u32[]{:S(2)}) collective-permute-start(f32[576,1,128]{0,2,1:T(8,128)S(1)} %slice.188), channel_id=1, source_target_pairs={{0,8},{8,16},{16,24},{1,9},{9,17},{17,25},{2,10},{10,18},{18,26},{... | collective-permute-start | bytes 884744 | tf_op jit(solution)/shard_map/ppermute | solution.py:30
  69.3 6.6 %collective-permute-start.9 = (f32[576,17,1]{0,2,1:T(1,128)S(1)}, f32[576,17,1]{0,2,1:T(1,128)S(1)}, u32[]{:S(2)}, u32[]{:S(2)}) collective-permute-start(f32[576,17,1]{0,2,1:T(1,128)S(1)} %pad_maximum_fusion.6), channel_id=1, source_target_pairs={{0,1},{1,2},{2,3},{3,4},{4,5},{5,6},{6,7},{8,9},{9,10},{10,11},{11... | collective-permute-start | bytes 117512 | tf_op jit(solution)/shard_map/ppermute | solution.py:30
  187.7 4.3 %collective-permute-start.11 = (f32[6,1,128]{2,0,1:T(8,128)S(1)}, f32[6,1,128]{2,0,1:T(8,128)S(1)}, u32[]{:S(2)}, u32[]{:S(2)}) collective-permute-start(f32[6,1,128]{2,0,1:T(8,128)S(1)} %get-tuple-element.51), channel_id=1, source_target_pairs={{8,0},{16,8},{24,16},{9,1},{17,9},{25,17},{10,2},{18,10},{26,18},{... | collective-permute-start | bytes 9224 | tf_op jit(solution)/shard_map/ppermute | solution.py:22
  189.0 3.8 %collective-permute-start.10 = (f32[6,1,128]{2,0,1:T(8,128)S(1)}, f32[6,1,128]{2,0,1:T(8,128)S(1)}, u32[]{:S(2)}, u32[]{:S(2)}) collective-permute-start(f32[6,1,128]{2,0,1:T(8,128)S(1)} %get-tuple-element.50), channel_id=1, source_target_pairs={{0,8},{8,16},{16,24},{1,9},{9,17},{17,25},{2,10},{10,18},{18,26},{... | collective-permute-start | bytes 9224 | tf_op jit(solution)/shard_map/ppermute | solution.py:21
  193.0 7.1 %collective-permute-start.12 = (f32[6,18,1]{2,0,1:T(8,128)S(1)}, f32[6,18,1]{2,0,1:T(8,128)S(1)}, u32[]{:S(2)}, u32[]{:S(2)}) collective-permute-start(f32[6,18,1]{2,0,1:T(8,128)S(1)} %get-tuple-element.39), channel_id=1, source_target_pairs={{0,1},{1,2},{2,3},{3,4},{4,5},{5,6},{6,7},{8,9},{9,10},{10,11},{11... | collective-permute-start | bytes 1304 | tf_op jit(solution)/shard_map/ppermute | solution.py:21
  197.3 7.0 %collective-permute-start.13 = (f32[6,18,1]{2,0,1:T(8,128)S(1)}, f32[6,18,1]{2,0,1:T(8,128)S(1)}, u32[]{:S(2)}, u32[]{:S(2)}) collective-permute-start(f32[6,18,1]{2,0,1:T(8,128)S(1)} %get-tuple-element.40), channel_id=1, source_target_pairs={{1,0},{2,1},{3,2},{4,3},{5,4},{6,5},{7,6},{9,8},{10,9},{11,10},{12... | collective-permute-start | bytes 1304 | tf_op jit(solution)/shard_map/ppermute | solution.py:22
  204.6 50.5 %copy-start.4 = (f32[6,16,128]{2,1,0:T(8,128)S(1)}, f32[6,16,128]{2,1,0:T(8,128)}, u32[]{:S(2)}) copy-start(f32[6,16,128]{2,1,0:T(8,128)} %param.10) | copy-start | bytes 147460
  204.6 50.5 %copy-start.6 = (f32[6,16,128]{2,1,0:T(8,128)S(1)}, f32[6,16,128]{2,1,0:T(8,128)}, u32[]{:S(2)}) copy-start(f32[6,16,128]{2,1,0:T(8,128)} %param.13) | copy-start | bytes 147460
  204.6 50.5 %copy-start.7 = (f32[6,16,128]{2,1,0:T(8,128)S(1)}, f32[6,16,128]{2,1,0:T(8,128)}, u32[]{:S(2)}) copy-start(f32[6,16,128]{2,1,0:T(8,128)} %param.11) | copy-start | bytes 147460
where the time goes:
time: 259 us; the launch traced here: 257 us
  blocking collectives  133 us (51%)
  starting transfers between devices  46.9 us (18%)
  local copies, waits for them, and re-layouts  34.5 us (13%)
  other arithmetic  20.9 us (8%)
  matrix products  9.44 us (4%)
  waiting for transfers between devices  7.56 us (3%)
  between operations  5.2 us (2%)
    psum x3, blocking collectives, global_sum(): return lax.psum(value, ('px', 'py'))  133 us
    ppermute x6, starting transfers between devices, with_halo(): before = lax.ppermute(last, axis, up)  21.8 us
    unnamed x31, local copies, waits for them, and re-layouts  16 us
    dot_general x2, other arithmetic, with_tangent(): return jnp.einsum('abxy,bxy->axy', extended, shells, precision=HIGH)  11.8 us
    all_to_all x1, starting transfers between devices, shards(): lax.all_to_all(held, ('px', 'py'), split_axis=1, concat_axis=1, tiled=True)  9.32 us
    ppermute x2, starting transfers between devices, shifted(): return lax.ppermute(shard, axis, pairs)  7.95 us
    ppermute x6, starting transfers between devices, with_halo(): after = lax.ppermute(leading, axis, down)  7.75 us
    scatter x1, local copies, waits for them, and re-layouts, shards(): contact_flat.at[:, targets]  6.65 us
  transfers between devices with their start and end apart: 15, of which 4 were waited for; matrix products, arithmetic and copies ran while one was open for 14% of the time, Pallas kernels for 0%

commit v1 on v0

v1 whole, which is shorter than its diff:
```python
import functools

import jax
import jax.numpy as jnp
from jax import lax
from jax.experimental import pallas as pl
from jax.experimental.pallas import tpu as pltpu
from jax.sharding import PartitionSpec as P

STEP = 0.2
MESH = pl.DeviceIdType.MESH
DIRS = ((1, 0), (-1, 0), (0, 1), (0, -1), (1, 1), (1, -1), (-1, 1), (-1, -1))
F32 = jnp.float32
BF16 = jnp.bfloat16


def up8(n):
    return (n + 7) // 8 * 8


def dot(a, b):
    return jnp.dot(a, b, preferred_element_type=F32)


def dot_t(a, b):
    return lax.dot_general(a, b, (((1,), (1,)), ((), ())), preferred_element_type=F32)


def split(x):
    hi = x.astype(BF16)
    return hi, (x - hi.astype(F32)).astype(BF16)


def kernel(
    npx, npy, cap,
    disp, vel, load, invm, hist_hbm, home_hbm, relaid_hbm, stiff, strain, table,
    spring, velout, hist_out, resid,
    relaid, hist, home, flat, send, recv, onehot, keep, soft, base,
    w1, w2, vm, ve, uf, y, ku, force, part, node, nodex, packed, halo_recv,
    red_send, red_recv,
    in_sem, out_sem, a_send, a_recv, h_send, h_recv, r_send, r_recv,
):
    n = npx * npy
    a = lax.axis_index("px")
    b = lax.axis_index("py")
    me = a * npy + b
    rows, cols = disp.shape[1], disp.shape[2]
    nh = strain.shape[0]
    capp = up8(cap)
    slots = n * capp
    pairs = rows // 2

    relaid_in = pltpu.make_async_copy(relaid_hbm, relaid, in_sem.at[0])
    hist_in = pltpu.make_async_copy(hist_hbm, hist, in_sem.at[1])
    home_in = pltpu.make_async_copy(home_hbm, home, in_sem.at[2])
    relaid_in.start()
    hist_in.start()
    home_in.start()

    def coords(t):
        return (lax.div(t, npy), lax.rem(t, npy))

    halo_recv[...] = jnp.zeros_like(halo_recv)
    recv[me] = jnp.zeros((capp, nh), F32)

    barrier = pltpu.get_barrier_semaphore()

    def greet(k, c):
        pl.semaphore_signal(
            barrier, inc=1, device_id=coords(lax.rem(me + k, n)), device_id_type=MESH
        )
        return c

    lax.fori_loop(1, n, greet, 0)

    lane = lax.broadcasted_iota(jnp.int32, (8, cols), 1)
    lane0 = lane == 0

    def exists(dx, dy):
        return (
            (a + dx >= 0) & (a + dx < npx) & (b + dy >= 0) & (b + dy < npy)
        )

    def halo_copy(e, t, src):
        dx, dy = DIRS[t]
        size = src.shape[0]
        return pltpu.make_async_remote_copy(
            src_ref=src,
            dst_ref=halo_recv.at[e, t, pl.ds(0, size)],
            send_sem=h_send.at[e, t],
            recv_sem=h_recv.at[e, t],
            device_id=(a + dx, b + dy),
            device_id_type=MESH,
        )

    def halo_start(e, items):
        for t, src in items:
            @pl.when(exists(*DIRS[t]))
            def _():
                halo_copy(e, t, src).start()

    def halo_recv_wait(e, items):
        for t, src in items:
            dx, dy = DIRS[t]

            @pl.when(exists(-dx, -dy))
            def _():
                halo_copy(e, t, src).wait_recv()

    def halo_send_wait(e, items):
        for t, src in items:
            @pl.when(exists(*DIRS[t]))
            def _():
                halo_copy(e, t, src).wait_send()

    node[...] = jnp.zeros_like(node)
    vm[...] = jnp.zeros_like(vm)
    for c in range(6):
        vm[0, pl.ds(c, rows, stride=8), :] = disp[c]
        vm[1, pl.ds(c, rows, stride=8), :] = load[c]
    ve[...] = jnp.zeros_like(ve)

    def column(ref, lead, count):
        total = jnp.zeros((8, cols), F32)
        for r in range(count):
            tile = ref[lead, pl.ds(8 * r, 8), :]
            moved = tile if r == 0 else pltpu.roll(tile, r, 1)
            total = jnp.where(lane == r, moved, total)
        return total

    for k in range(2):
        packed[0, 0, pl.ds(8 * k, 8), :] = column(vm, k, rows)
        packed[0, 1, pl.ds(8 * k, 8), :] = vm[k, pl.ds(0, 8), :]

    relaid_in.wait()
    flat[pl.ds(0, n * cap), :] = jnp.transpose(relaid[...])
    for r in range(n * cap, flat.shape[0], 8):
        flat[pl.ds(r, 8), :] = jnp.zeros((8, nh), F32)
    for d in range(n):
        send[d] = flat[pl.ds(d * cap, capp), :]

    pl.semaphore_wait(barrier, n - 1)

    ex0 = [(1, packed.at[0, 1]), (3, packed.at[0, 0]), (7, packed.at[0, 1])]
    halo_start(0, ex0)

    def a2a(target, slot, source):
        return pltpu.make_async_remote_copy(
            src_ref=send.at[slot],
            dst_ref=recv.at[source],
            send_sem=a_send.at[slot],
            recv_sem=a_recv.at[source],
            device_id=coords(target),
            device_id_type=MESH,
        )

    def a2a_start(k, c):
        target = lax.rem(me + k, n)
        a2a(target, target, me).start()
        return c

    lax.fori_loop(1, n, a2a_start, 0)

    def picks(shape, row_dim, shift):
        k = lax.broadcasted_iota(jnp.int32, shape, row_dim)
        m = lax.broadcasted_iota(jnp.int32, shape, 1 - row_dim)
        c = lax.div(k, 6)
        place = 8 * c + (k - 6 * c)
        hit = m == place + shift[0]
        for s in shift[1:]:
            hit = hit | (m == place + s)
        return jnp.where(hit, 1.0, 0.0).astype(BF16)

    sel_hi = picks((24, 96), 0, (0, 32))
    sel_lo = picks((24, 96), 0, (64,))
    sel_rows = picks((32, 24), 1, (0,))
    bh, bl = split(strain[...])
    kh, kl = split(stiff[...])
    kh = dot(sel_rows, kh).astype(BF16)
    kl = dot(sel_rows, kl).astype(BF16)
    w1[pl.ds(0, nh), :] = (dot(bh, sel_hi) + dot(bl, sel_lo)).astype(BF16)
    w1[pl.ds(nh, 32), :] = (dot(kh, sel_hi) + dot(kl, sel_lo)).astype(BF16)
    bth = dot_t(sel_rows, bh).astype(BF16)
    btl = dot_t(sel_rows, bl).astype(BF16)
    w2[...] = jnp.concatenate([bth, bth, btl], axis=1)

    last_row = a == npx - 1
    last_col = b == npy - 1

    def gather(mref, lead, eref):
        def row(r):
            m = mref[lead, pl.ds(8 * r, 8), :]
            e = eref[lead, pl.ds(8 * r, 8), :]
            return m, pltpu.roll(jnp.where(lane0, e, m), cols - 1, 1)

        prev = row(0)
        for p in range(pairs):
            us = []
            for r in (2 * p, 2 * p + 1):
                nxt = row(r + 1)
                u = jnp.concatenate([prev[0], nxt[0], prev[1], nxt[1]], axis=0)
                uf[r] = u
                us.append(u)
                prev = nxt
            u = jnp.concatenate(us, axis=1)
            uh, ul = split(u)
            out = dot(w1[...], jnp.concatenate([uh, ul, uh], axis=0))
            y[p] = out[:nh]
            ku[p] = out[nh:]

    def assemble(e, get):
        below = None
        for r in range(rows + 1):
            main = jnp.zeros((8, cols), F32)
            shift = jnp.zeros((8, cols), F32)
            if r > 0:
                main, shift = below
            if r < rows:
                f = get(r)
                main = main + f[0:8]
                shift = shift + f[16:24]
                below = (f[8:16], f[24:32])
            rolled = pltpu.roll(shift, 1, 1)
            part[e, r, pl.ds(0, 8), :] = main + jnp.where(lane0, 0.0, rolled)
            part[e, r, pl.ds(8, 8), :] = jnp.where(lane0, rolled, 0.0)

    def part_column(e, off):
        total = jnp.zeros((8, cols), F32)
        for r in range(rows + 1):
            tile = part[e, r, pl.ds(off, 8), :]
            moved = tile if r == 0 else pltpu.roll(tile, r, 1)
            total = jnp.where(lane == r, moved, total)
        return total

    def exchange_items(e):
        return [
            (0, part.at[e, rows]),
            (1, part.at[e, 0]),
            (2, packed.at[e + 1, 0, pl.ds(0, 8)]),
            (3, packed.at[e + 1, 0, pl.ds(8, 8)]),
            (4, part.at[e, rows, pl.ds(8, 8)]),
            (5, part.at[e, rows, pl.ds(0, 8)]),
            (6, part.at[e, 0, pl.ds(8, 8)]),
            (7, part.at[e, 0, pl.ds(0, 8)]),
        ]

    def exchange_start(e):
        packed[e + 1, 0, pl.ds(0, 8), :] = part_column(e, 8)
        packed[e + 1, 0, pl.ds(8, 8), :] = part_column(e, 0)
        items = exchange_items(e)
        halo_start(e + 1, items)
        return items

    def got(e, t, off=0):
        return halo_recv[e, t, pl.ds(off, 8), :]

    def at0(x):
        return jnp.where(lane0, x, 0.0)

    def exchange_finish(e, items, put):
        halo_recv_wait(e + 1, items)
        from_prev = got(e + 1, 2)
        from_next = got(e + 1, 3)
        for r in range(rows + 1):
            main = part[e, r, pl.ds(0, 8), :]
            extra = part[e, r, pl.ds(8, 8), :]
            sh = (cols - r) % cols
            pv = from_prev if r == 0 else pltpu.roll(from_prev, sh, 1)
            nx = from_next if r == 0 else pltpu.roll(from_next, sh, 1)
            main = main + at0(pv)
            extra = extra + at0(nx)
            if r == 0:
                main = main + got(e + 1, 0) + at0(got(e + 1, 4))
                extra = extra + got(e + 1, 0, 8) + at0(got(e + 1, 5))
            if r == rows:
                main = main + got(e + 1, 1) + at0(got(e + 1, 6))
                extra = extra + got(e + 1, 1, 8) + at0(got(e + 1, 7))
                main = jnp.where(last_row, 0.0, main)
                extra = jnp.where(last_row, 0.0, extra)
            put(r, main, jnp.where(last_col, 0.0, extra))

    halo_recv_wait(0, ex0)
    for k in range(2):
        vm[k, pl.ds(8 * rows, 8), :] = got(0, 1, 8 * k)
        col = got(0, 3, 8 * k)
        for r in range(rows):
            moved = col if r == 0 else pltpu.roll(col, cols - r, 1)
            ve[k, pl.ds(8 * r, 8), :] = at0(moved)
        ve[k, pl.ds(8 * rows, 8), :] = at0(got(0, 7, 8 * k))

    gather(vm, 0, ve)
    assemble(0, lambda r: ku[r // 2, :, pl.ds(cols * (r % 2), cols)])
    items0 = exchange_start(0)

    hist_in.wait()
    for r in range(rows):
        h = hist[pl.ds(r, nh, stride=rows), :] + y[r // 2, :, pl.ds(cols * (r % 2), cols)]
        hist[pl.ds(r, nh, stride=rows), :] = h
        soft[r // 2, :, pl.ds(cols * (r % 2), cols)] = (
            jnp.maximum(h, 0.0) + jnp.log1p(jnp.exp(-jnp.abs(h)))
        )
    hist_write = pltpu.make_async_copy(hist, hist_out, out_sem.at[0])
    hist_write.start()

    def put_rhs(r, main, extra):
        m = vm[1, pl.ds(8 * r, 8), :] - main
        e = ve[1, pl.ds(8 * r, 8), :] - extra
        node[0, pl.ds(8 * r, 8), :] = m
        nodex[0, pl.ds(8 * r, 8), :] = e

    exchange_finish(0, items0, put_rhs)
    gather(node, 0, nodex)

    rr = jnp.zeros((8, cols), F32)
    for r in range(rows):
        m = node[0, pl.ds(8 * r, 8), :]
        rr = rr + m * m

    for c in range(6):
        r0 = node[0, pl.ds(c, rows, stride=8), :]
        v = vel[c] + STEP * invm[c] * r0
        velout[c] = v
        spring[c] = disp[c] + STEP * v

    place = jnp.broadcast_to(table[...].astype(F32), (nh, n * cap))
    flat[pl.ds(0, n * cap), :] = jnp.transpose(place)
    sub = lax.broadcasted_iota(jnp.int32, (capp, nh), 0)
    lanes = lax.broadcasted_iota(jnp.int32, (capp, nh), 1).astype(F32)
    for d in range(n):
        t = flat[pl.ds(d * cap, capp), :]
        keep[pl.ds(d * capp, capp), :] = jnp.where(
            sub < cap, t - lanes, float(rows * cols)
        )

    ones = jnp.ones((16, slots), BF16)
    home_in.wait()

    def build(p, c):
        for half in range(2):
            lo = (2 * p + half) * cols
            at = lo.astype(F32)
            for s in range(0, slots, 128):
                hit = jnp.where(keep[pl.ds(s, 128), :] == at, 1.0, 0.0)
                onehot[p, pl.ds(s, 128), pl.ds(half * cols, cols)] = hit.astype(BF16)
        mask = dot(ones, onehot[p])[0:1, :]
        stay = 1.0 - mask
        own = jnp.concatenate(
            [home[pl.ds(2 * p + half, nh, stride=rows), :] for half in range(2)], axis=1
        )
        base[p] = soft[p] * own * stay
        return c

    lax.fori_loop(0, pairs, build, 0)

    def a2a_wait(k, c):
        source = lax.rem(me + k, n)
        a2a(me, source, source).wait_recv()
        return c

    lax.fori_loop(1, n, a2a_wait, 0)
    got_all = jnp.transpose(recv[...].reshape(slots, nh))
    ch, cl = split(got_all)
    both = jnp.concatenate([ch, cl], axis=0)

    def push(z, p):
        zh, zl = split(z)
        f = dot(w2[...], jnp.concatenate([zh, zl, zh], axis=0)) + ku[p]
        force[2 * p] = f[:, :cols]
        force[2 * p + 1] = f[:, cols:]

    for p in range(pairs):
        m = dot(both, onehot[p])
        w = base[p] + soft[p] * (m[:nh] + m[nh:])
        base[p] = w
        push(w * y[p], p)

    assemble(1, lambda r: force[r])
    items1 = exchange_start(1)

    def energy():
        total = jnp.zeros((8, cols), F32)
        for r in range(rows):
            prod = uf[r] * force[r]
            total = total + ((prod[0:8] + prod[8:16]) + (prod[16:24] + prod[24:32]))
        return total

    ru = energy()

    def put_u1(r, main, extra):
        node[1, pl.ds(8 * r, 8), :] = main
        nodex[1, pl.ds(8 * r, 8), :] = extra

    exchange_finish(1, items1, put_u1)
    gather(node, 1, nodex)
    uu = jnp.zeros((8, cols), F32)
    for r in range(rows):
        m = node[1, pl.ds(8 * r, 8), :]
        uu = uu + m * m
    for p in range(pairs):
        push(base[p] * y[p], p)
    uv = energy()

    def fold(x):
        return jnp.sum(x, axis=0, keepdims=True)

    zero = jnp.zeros((4, cols), F32)
    mine = jnp.concatenate([fold(rr), fold(ru), fold(uu), fold(uv), zero], axis=0)
    red_send[...] = mine
    red_recv[me] = mine

    def red(target, source):
        return pltpu.make_async_remote_copy(
            src_ref=red_send,
            dst_ref=red_recv.at[source],
            send_sem=r_send.at[target],
            recv_sem=r_recv.at[source],
            device_id=coords(target),
            device_id_type=MESH,
        )

    def red_start(k, c):
        red(lax.rem(me + k, n), me).start()
        return c

    lax.fori_loop(1, n, red_start, 0)

    assemble(2, lambda r: force[r])
    packed[3, 0, pl.ds(0, 8), :] = part_column(2, 8)
    all2 = exchange_items(2)
    items2 = [all2[0], all2[2], all2[4]]
    halo_start(3, items2)
    halo_recv_wait(3, items2)
    from_prev = got(3, 2)
    for r in range(rows):
        main = part[2, r, pl.ds(0, 8), :]
        pv = from_prev if r == 0 else pltpu.roll(from_prev, cols - r, 1)
        main = main + at0(pv)
        if r == 0:
            main = main + got(3, 0) + at0(got(3, 4))
        node[2, pl.ds(8 * r, 8), :] = main

    def red_wait(k, c):
        source = lax.rem(me + k, n)
        red(source, source).wait_recv()
        return c

    lax.fori_loop(1, n, red_wait, 0)
    total = jnp.sum(red_recv[...], axis=0)
    sums = jnp.broadcast_to(jnp.sum(total, axis=1, keepdims=True), (8, cols))
    s_rr, s_ru, s_uu, s_uv = (sums[k : k + 1, :] for k in range(4))
    alpha = s_rr / s_ru
    new = s_rr + alpha * (alpha * s_uu - 2.0 * s_ru)
    grow = 1.0 + new / s_rr
    curve = grow * (grow * s_ru - 2.0 * alpha * s_uu) + alpha * alpha * s_uv
    beta = new / curve
    x_r = alpha + beta * grow
    x_u = -beta * alpha
    r_u = -(alpha + beta * grow)
    r_v = beta * alpha
    for c in range(6):
        r0 = node[0, pl.ds(c, rows, stride=8), :]
        u1 = node[1, pl.ds(c, rows, stride=8), :]
        u2 = node[2, pl.ds(c, rows, stride=8), :]
        spring[c] = spring[c] + x_r * r0 + x_u * u1
        resid[c] = r0 + r_u * u1 + r_v * u2

    hist_write.wait()
    halo_send_wait(0, ex0)
    halo_send_wait(1, items0)
    halo_send_wait(2, items1)
    halo_send_wait(3, items2)

    def drain(k, c):
        target = lax.rem(me + k, n)
        a2a(target, target, me).wait_send()
        red(target, me).wait_send()
        return c

    lax.fori_loop(1, n, drain, 0)


def shards(
    npx, npy,
    displacement, velocity, load, inv_mass, history, contact_home, recv_contact,
    stiff_base, strain_map, slot_table,
):
    nh, rows, cols = history.shape
    n = npx * npy
    width = recv_contact.shape[-1]
    cap = width // n
    capp = up8(cap)
    slots = n * capp
    cells = rows * cols
    pairs = rows // 2
    field = jax.ShapeDtypeStruct(displacement.shape, F32)
    vmem = pl.BlockSpec(memory_space=pltpu.VMEM)
    hbm = pl.BlockSpec(memory_space=pl.ANY)
    nodes = 8 * (rows + 1)
    dma = pltpu.SemaphoreType.DMA
    out = pl.pallas_call(
        functools.partial(kernel, npx, npy, cap),
        out_shape=(field, field, jax.ShapeDtypeStruct((nh * rows, cols), F32), field),
        in_specs=[vmem, vmem, vmem, vmem, hbm, hbm, hbm, vmem, vmem, vmem],
        out_specs=(vmem, vmem, hbm, vmem),
        scratch_shapes=[
            pltpu.VMEM((nh, width), F32),
            pltpu.VMEM((nh * rows, cols), F32),
            pltpu.VMEM((nh * rows, cols), F32),
            pltpu.VMEM((width + capp, nh), F32),
            pltpu.VMEM((n, capp, nh), F32),
            pltpu.VMEM((n, capp, nh), F32),
            pltpu.VMEM((pairs, slots, 2 * cols), BF16),
            pltpu.VMEM((slots, nh), F32),
            pltpu.VMEM((pairs, nh, 2 * cols), F32),
            pltpu.VMEM((pairs, nh, 2 * cols), F32),
            pltpu.VMEM((nh + 32, 96), BF16),
            pltpu.VMEM((32, 3 * nh), BF16),
            pltpu.VMEM((2, nodes, cols), F32),
            pltpu.VMEM((2, nodes, cols), F32),
            pltpu.VMEM((rows, 32, cols), F32),
            pltpu.VMEM((pairs, nh, 2 * cols), F32),
            pltpu.VMEM((pairs, 32, 2 * cols), F32),
            pltpu.VMEM((rows, 32, cols), F32),
            pltpu.VMEM((3, rows + 1, 16, cols), F32),
            pltpu.VMEM((3, nodes, cols), F32),
            pltpu.VMEM((2, nodes, cols), F32),
            pltpu.VMEM((4, 2, 16, cols), F32),
            pltpu.VMEM((4, 8, 16, cols), F32),
            pltpu.VMEM((8, cols), F32),
            pltpu.VMEM((n, 8, cols), F32),
            dma((3,)),
            dma((1,)),
            dma((n,)),
            dma((n,)),
            dma((4, 8)),
            dma((4, 8)),
            dma((n,)),
            dma((n,)),
        ],
        compiler_params=pltpu.CompilerParams(
            collective_id=0, has_side_effects=True, vmem_limit_bytes=48 << 20
        ),
        name="springback",
    )(
        displacement, velocity, load, inv_mass,
        history.reshape(nh * rows, cols), contact_home.reshape(nh * rows, cols),
        recv_contact.reshape(nh, width), stiff_base, strain_map,
        slot_table.reshape(1, width),
    )
    return (out[0], out[1], out[2].reshape(nh, rows, cols), out[3])


def solution(mesh):
    field = P(None, "px", "py")
    return jax.shard_map(
        functools.partial(shards, mesh.shape["px"], mesh.shape["py"]),
        mesh=mesh,
        in_specs=(field,) * 6 + (P("px", "py", None, None), P(), P(), P("px", "py", None)),
        out_specs=(field,) * 4,
        check_vma=False,
    )
```

time: 259 us -> 49.7 us (0.19)
  blocking collectives: 133 us -> 0 us
  starting transfers between devices: 46.9 us -> 0 us
  Pallas kernels: 0 us -> 42.4 us
  local copies, waits for them, and re-layouts: 34.5 us -> 6.31 us
  other arithmetic: 20.9 us -> 0 us
  matrix products: 9.44 us -> 0 us
  waiting for transfers between devices: 7.56 us -> 0 us
  between operations: 5.2 us -> 0.77 us
    psum x3 -> x0, blocking collectives: 133 us -> none  [global_sum(): return lax.psum(value, ('px', 'py'))]
    pallas_call x0 -> x1, Pallas kernels: none -> 42.4 us  [shards(): pl.pallas_call(functools.partial(kernel, npx, npy, cap), out_shape=(field...]
    ppermute x14 -> x0, starting transfers between devices: 37.5 us -> none  [the longest x6 21.8 us: with_halo(): before = lax.ppermute(last, axis, up)]
    dot_general x2 -> x0, other arithmetic: 11.8 us -> none  [with_tangent(): return jnp.einsum('abxy,bxy->axy', extended, shells, precision=HIGH)]
    unnamed x31 -> x22, local copies, waits for them, and re-layouts: 16 us -> 6.31 us
    dot_general x3 -> x0, matrix products: 9.44 us -> none  [the longest x1 5.96 us: shards(): jnp.dot(pairs.T, weights, precision=HIGH)]
    all_to_all x1 -> x0, starting transfers between devices: 9.32 us -> none  [shards(): lax.all_to_all(held, ('px', 'py'), split_axis=1, concat_axis=1, tiled=True)]
    reshape x3 -> x0, local copies, waits for them, and re-layouts: 8.85 us -> none  [the longest x1 5.76 us: shards(): tangent = tangent.reshape(576, rows, cols)]
  transfers between devices with their start and end apart: 15 -> 0, of which waited for: 4 -> 0; matrix products, arithmetic and copies ran while one was open for 14% -> 0% of each run, Pallas kernels for 0% -> 0%
where the time goes in v1:
time: 49.7 us; the launch traced here: 49.4 us
  Pallas kernels  42.4 us (85%)
  local copies, waits for them, and re-layouts  6.31 us (13%)
  between operations  0.77 us (2%)
    pallas_call x1, Pallas kernels, shards(): pl.pallas_call(functools.partial(kernel, npx, npy, cap), out_shape=(field...  42.4 us
    unnamed x22, local copies, waits for them, and re-layouts  6.31 us

profile of v1, /device:TPU:0, one launch (start us, length us, event | category | flops | bytes accessed | tf_op | source)
XLA Modules:
  0.0 49.4 jit_solution(7917277507618155169)
XLA Ops:
  0.6 0.0 copy-start
  0.6 0.9 %copy.15.strain = f32[128,24]{1,0:T(8,128)S(1)} copy(f32[128,24]{0,1:T(8,128)} %param.18) | data formatting | bytes 24576 | tf_op args[8]
  1.5 0.0 copy-start.2
  1.5 0.0 copy-start.3
  1.6 0.0 copy-start.4
  1.6 0.0 copy-start.5
  1.6 0.0 copy-start.6
  1.6 0.0 copy-start.7
  1.6 1.3 %copy.14 = f32[1,1,128,1216]{3,2,1,0:T(8,128)S(1)} copy(f32[1,1,128,1216]{2,3,1,0:T(8,128)} %param.16) | data formatting | bytes 1245184 | tf_op args[6]
  2.9 0.0 copy-done
  3.0 0.0 copy-done.2
  3.0 0.0 copy-done.3
  3.0 0.0 copy-done.4
  3.0 0.0 copy-done.5
  3.0 0.0 copy-done.6
  3.0 0.0 copy-done.7
  3.0 0.0 copy-start.1
  3.0 1.2 %copy-done.1 = f32[128,16,128]{2,1,0:T(8,128)S(1)} copy-done((f32[128,16,128]{2,1,0:T(8,128)S(1)}, f32[128,16,128]{2,1,0:T(8,128)}, u32[]{:S(2)}) %copy-start.1) | copy-done | bytes 1048600
  4.2 42.4 %springback.1 = (f32[6,16,128]{2,1,0:T(8,128)S(1)}, f32[6,16,128]{2,1,0:T(8,128)S(1)}, f32[2048,128]{1,0:T(8,128)S(1)}, f32[6,16,128]{2,1,0:T(8,128)S(1)}) custom-call(f32[6,16,128]{2,1,0:T(8,128)S(1)} %copy-done.2, f32[6,16,128]{2,1,0:T(8,128)S(1)} %copy-done.3, f32[6,16,128]{2,1,0:T(8,128)S(1)} %copy-done.4, f32[6,16,128]{2,1,0:T(8,128)S(1)} %copy-done.5, ...), custom_call_target="tpu_custom_call" | custom-call | tf_op jit(solution)/shard_map/springback/pallas_call | solution.py:500
  46.6 0.6 %copy.20 = f32[6,16,128]{2,1,0:T(8,128)} copy(f32[6,16,128]{2,1,0:T(8,128)S(1)} %get-tuple-element.16) | data formatting | bytes 98304
  47.2 0.6 %copy.21 = f32[6,16,128]{2,1,0:T(8,128)} copy(f32[6,16,128]{2,1,0:T(8,128)S(1)} %get-tuple-element.17) | data formatting | bytes 98304
  47.8 1.0 %copy.22 = f32[128,16,128]{2,1,0:T(8,128)} copy(f32[128,16,128]{2,1,0:T(8,128)S(1)} %bitcast.8) | data formatting | bytes 2097152
  48.8 0.6 %copy.23 = f32[6,16,128]{2,1,0:T(8,128)} copy(f32[6,16,128]{2,1,0:T(8,128)S(1)} %get-tuple-element.19) | data formatting | bytes 98304
Async XLA Ops:
  0.6 2.3 %copy-start = (f32[128,16,128]{2,1,0:T(8,128)S(1)}, f32[128,16,128]{2,1,0:T(8,128)}, u32[]{:S(2)}) copy-start(f32[128,16,128]{2,1,0:T(8,128)} %param.14) | copy-start | bytes 3145732
  1.5 1.4 %copy-start.2 = (f32[6,16,128]{2,1,0:T(8,128)S(1)}, f32[6,16,128]{2,1,0:T(8,128)}, u32[]{:S(2)}) copy-start(f32[6,16,128]{2,1,0:T(8,128)} %disp.1) | copy-start | bytes 147460
  1.5 1.4 %copy-start.3 = (f32[6,16,128]{2,1,0:T(8,128)S(1)}, f32[6,16,128]{2,1,0:T(8,128)}, u32[]{:S(2)}) copy-start(f32[6,16,128]{2,1,0:T(8,128)} %vel.1) | copy-start | bytes 147460
  1.6 1.4 %copy-start.4 = (f32[6,16,128]{2,1,0:T(8,128)S(1)}, f32[6,16,128]{2,1,0:T(8,128)}, u32[]{:S(2)}) copy-start(f32[6,16,128]{2,1,0:T(8,128)} %load.1) | copy-start | bytes 147460
  1.6 1.4 %copy-start.5 = (f32[6,16,128]{2,1,0:T(8,128)S(1)}, f32[6,16,128]{2,1,0:T(8,128)}, u32[]{:S(2)}) copy-start(f32[6,16,128]{2,1,0:T(8,128)} %invm.1) | copy-start | bytes 147460
  1.6 1.4 %copy-start.6 = (f32[24,24]{1,0:T(8,128)S(1)}, f32[24,24]{1,0:T(8,128)}, u32[]{:S(2)}) copy-start(f32[24,24]{1,0:T(8,128)} %stiff.1) | copy-start | bytes 6916
  1.6 1.4 %copy-start.7 = (s32[1,1,1216]{2,1,0:T(1,128)S(1)}, s32[1,1,1216]{2,1,0:T(1,128)}, u32[]{:S(2)}) copy-start(s32[1,1,1216]{2,1,0:T(1,128)} %param.19) | copy-start | bytes 14596
  3.0 1.2 %copy-start.1 = (f32[128,16,128]{2,1,0:T(8,128)S(1)}, f32[128,16,128]{2,1,0:T(8,128)}, u32[]{:S(2)}) copy-start(f32[128,16,128]{2,1,0:T(8,128)} %param.15) | copy-start | bytes 3145732

commit v2 on v1

--- a/solution.py
+++ b/solution.py
@@ -22,10 +22,6 @@
     return jnp.dot(a, b, preferred_element_type=F32)
 
 
-def dot_t(a, b):
-    return lax.dot_general(a, b, (((1,), (1,)), ((), ())), preferred_element_type=F32)
-
-
 def split(x):
     hi = x.astype(BF16)
     return hi, (x - hi.astype(F32)).astype(BF16)
@@ -33,35 +29,49 @@
 
 def kernel(
     npx, npy, cap,
-    disp, vel, load, invm, hist_hbm, home_hbm, relaid_hbm, stiff, strain, table,
+    disp_hbm, vel_hbm, load_hbm, invm_hbm, hist_hbm, home_hbm, relaid_hbm, stiff_hbm,
+    strain_hbm, table_hbm,
     spring, velout, hist_out, resid,
+    disp, vel, load, invm, stiff, strain, table,
     relaid, hist, home, flat, send, recv, onehot, keep, soft, base,
     w1, w2, vm, ve, uf, y, ku, force, part, node, nodex, packed, halo_recv,
     red_send, red_recv,
-    in_sem, out_sem, a_send, a_recv, h_send, h_recv, r_send, r_recv,
+    in_sem, a_send, a_recv, h_send, h_recv, r_send, r_recv,
 ):
     n = npx * npy
     a = lax.axis_index("px")
     b = lax.axis_index("py")
     me = a * npy + b
     rows, cols = disp.shape[1], disp.shape[2]
-    nh = strain.shape[0]
+    nh = strain.shape[1]
     capp = up8(cap)
     slots = n * capp
     pairs = rows // 2
 
-    relaid_in = pltpu.make_async_copy(relaid_hbm, relaid, in_sem.at[0])
-    hist_in = pltpu.make_async_copy(hist_hbm, hist, in_sem.at[1])
-    home_in = pltpu.make_async_copy(home_hbm, home, in_sem.at[2])
+    width = n * cap
+    relaid_in = pltpu.make_async_copy(
+        relaid_hbm, relaid.at[pl.ds(0, width)], in_sem.at[0]
+    )
+    others = [
+        pltpu.make_async_copy(src, dst, in_sem.at[k + 1])
+        for k, (src, dst) in enumerate((
+            (disp_hbm, disp), (load_hbm, load), (strain_hbm, strain), (stiff_hbm, stiff),
+            (hist_hbm, hist), (vel_hbm, vel), (invm_hbm, invm), (table_hbm, table),
+            (home_hbm, home),
+        ))
+    ]
+    (disp_in, load_in, strain_in, stiff_in, hist_in, vel_in, invm_in, table_in,
+     home_in) = others
     relaid_in.start()
-    hist_in.start()
-    home_in.start()
+    for copy in others:
+        copy.start()
 
     def coords(t):
         return (lax.div(t, npy), lax.rem(t, npy))
 
     halo_recv[...] = jnp.zeros_like(halo_recv)
-    recv[me] = jnp.zeros((capp, nh), F32)
+    here = (npy - 1) * npx
+    recv[here] = jnp.zeros((capp, nh), F32)
 
     barrier = pltpu.get_barrier_semaphore()
 
@@ -115,6 +125,8 @@
 
     node[...] = jnp.zeros_like(node)
     vm[...] = jnp.zeros_like(vm)
+    disp_in.wait()
+    load_in.wait()
     for c in range(6):
         vm[0, pl.ds(c, rows, stride=8), :] = disp[c]
         vm[1, pl.ds(c, rows, stride=8), :] = load[c]
@@ -132,34 +144,50 @@
         packed[0, 0, pl.ds(8 * k, 8), :] = column(vm, k, rows)
         packed[0, 1, pl.ds(8 * k, 8), :] = vm[k, pl.ds(0, 8), :]
 
+    for r in range(width, relaid.shape[0], 8):
+        relaid[pl.ds(r, 8), :] = jnp.zeros((8, nh), F32)
     relaid_in.wait()
-    flat[pl.ds(0, n * cap), :] = jnp.transpose(relaid[...])
-    for r in range(n * cap, flat.shape[0], 8):
-        flat[pl.ds(r, 8), :] = jnp.zeros((8, nh), F32)
     for d in range(n):
-        send[d] = flat[pl.ds(d * cap, capp), :]
+        send[d] = relaid[pl.ds(d * cap, capp), :]
 
     pl.semaphore_wait(barrier, n - 1)
 
     ex0 = [(1, packed.at[0, 1]), (3, packed.at[0, 0]), (7, packed.at[0, 1])]
     halo_start(0, ex0)
 
-    def a2a(target, slot, source):
+    def offset(q):
+        r, da = lax.div(q, npx), lax.rem(q, npx)
+        odd = lax.rem(r, 2)
+        ds = npy // 2 + (1 - 2 * odd) * lax.div(r + 1, 2)
+        return da, lax.rem(ds + npy, npy)
+
+    def a2a(q):
+        da, ds = offset(q)
+        ta, tb = lax.rem(a + da, npx), lax.rem(b + ds, npy)
         return pltpu.make_async_remote_copy(
-            src_ref=send.at[slot],
-            dst_ref=recv.at[source],
-            send_sem=a_send.at[slot],
-            recv_sem=a_recv.at[source],
-            device_id=coords(target),
+            src_ref=send.at[ta * npy + tb],
+            dst_ref=recv.at[q],
+            send_sem=a_send.at[q],
+            recv_sem=a_recv.at[q],
+            device_id=(ta, tb),
             device_id_type=MESH,
         )
 
-    def a2a_start(k, c):
-        target = lax.rem(me + k, n)
-        a2a(target, target, me).start()
-        return c
-
-    lax.fori_loop(1, n, a2a_start, 0)
+    def source_of(q):
+        da, ds = offset(q)
+        return lax.rem(a - da + npx, npx) * npy + lax.rem(b - ds + npy, npy)
+
+    def a2a_start(q, c):
+        a2a(q).start()
+        return c
+
+    def each(lo, hi, body):
+        if lo < min(hi, here):
+            lax.fori_loop(lo, min(hi, here), body, 0)
+        if max(lo, here + 1) < hi:
+            lax.fori_loop(max(lo, here + 1), hi, body, 0)
+
+    each(0, n, a2a_start)
 
     def picks(shape, row_dim, shift):
         k = lax.broadcasted_iota(jnp.int32, shape, row_dim)
@@ -174,14 +202,17 @@
     sel_hi = picks((24, 96), 0, (0, 32))
     sel_lo = picks((24, 96), 0, (64,))
     sel_rows = picks((32, 24), 1, (0,))
-    bh, bl = split(strain[...])
+    strain_in.wait()
+    stiff_in.wait()
+    bth, btl = split(strain[...])
+    bh, bl = split(jnp.transpose(strain[...]))
     kh, kl = split(stiff[...])
     kh = dot(sel_rows, kh).astype(BF16)
     kl = dot(sel_rows, kl).astype(BF16)
     w1[pl.ds(0, nh), :] = (dot(bh, sel_hi) + dot(bl, sel_lo)).astype(BF16)
     w1[pl.ds(nh, 32), :] = (dot(kh, sel_hi) + dot(kl, sel_lo)).astype(BF16)
-    bth = dot_t(sel_rows, bh).astype(BF16)
-    btl = dot_t(sel_rows, bl).astype(BF16)
+    bth = dot(sel_rows, bth).astype(BF16)
+    btl = dot(sel_rows, btl).astype(BF16)
     w2[...] = jnp.concatenate([bth, bth, btl], axis=1)
 
     last_row = a == npx - 1
@@ -299,7 +330,8 @@
         soft[r // 2, :, pl.ds(cols * (r % 2), cols)] = (
             jnp.maximum(h, 0.0) + jnp.log1p(jnp.exp(-jnp.abs(h)))
         )
-    hist_write = pltpu.make_async_copy(hist, hist_out, out_sem.at[0])
+
+    hist_write = pltpu.make_async_copy(hist, hist_out, in_sem.at[10])
     hist_write.start()
 
     def put_rhs(r, main, extra):
@@ -316,21 +348,30 @@
         m = node[0, pl.ds(8 * r, 8), :]
         rr = rr + m * m
 
+    vel_in.wait()
+    invm_in.wait()
     for c in range(6):
         r0 = node[0, pl.ds(c, rows, stride=8), :]
         v = vel[c] + STEP * invm[c] * r0
         velout[c] = v
         spring[c] = disp[c] + STEP * v
 
+    table_in.wait()
     place = jnp.broadcast_to(table[...].astype(F32), (nh, n * cap))
     flat[pl.ds(0, n * cap), :] = jnp.transpose(place)
     sub = lax.broadcasted_iota(jnp.int32, (capp, nh), 0)
     lanes = lax.broadcasted_iota(jnp.int32, (capp, nh), 1).astype(F32)
-    for d in range(n):
-        t = flat[pl.ds(d * cap, capp), :]
-        keep[pl.ds(d * capp, capp), :] = jnp.where(
+    for r in range(n * cap, flat.shape[0], 8):
+        flat[pl.ds(r, 8), :] = jnp.zeros((8, nh), F32)
+
+    def arrange(q, c):
+        t = flat[pl.ds(source_of(q) * cap, capp), :]
+        keep[pl.ds(pl.multiple_of(q * capp, 8), capp), :] = jnp.where(
             sub < cap, t - lanes, float(rows * cols)
         )
+        return c
+
+    lax.fori_loop(0, n, arrange, 0)
 
     ones = jnp.ones((16, slots), BF16)
     home_in.wait()
@@ -352,15 +393,24 @@
 
     lax.fori_loop(0, pairs, build, 0)
 
-    def a2a_wait(k, c):
-        source = lax.rem(me + k, n)
-        a2a(me, source, source).wait_recv()
-        return c
-
-    lax.fori_loop(1, n, a2a_wait, 0)
-    got_all = jnp.transpose(recv[...].reshape(slots, nh))
-    ch, cl = split(got_all)
-    both = jnp.concatenate([ch, cl], axis=0)
+    def a2a_wait(q, c):
+        a2a(q).wait_recv()
+        return c
+
+    late = n - 2 * nh // capp // 2 * 2
+
+    def arrived(lo, hi):
+        each(lo, hi, a2a_wait)
+        size = (hi - lo) * capp
+        got_all = jnp.transpose(recv[pl.ds(lo, hi - lo)].reshape(size, nh))
+        ch, cl = split(got_all)
+        return jnp.concatenate([ch, cl], axis=0)
+
+    both = arrived(0, late)
+    for p in range(pairs):
+        m = dot(both, onehot[p, pl.ds(0, late * capp), :])
+        base[p] = base[p] + soft[p] * (m[:nh] + m[nh:])
+    both = arrived(late, n)
 
     def push(z, p):
         zh, zl = split(z)
@@ -369,7 +419,7 @@
         force[2 * p + 1] = f[:, cols:]
 
     for p in range(pairs):
-        m = dot(both, onehot[p])
+        m = dot(both, onehot[p, pl.ds(late * capp, slots - late * capp), :])
         w = base[p] + soft[p] * (m[:nh] + m[nh:])
         base[p] = w
         push(w * y[p], p)
@@ -471,12 +521,37 @@
     halo_send_wait(3, items2)
 
     def drain(k, c):
-        target = lax.rem(me + k, n)
-        a2a(target, target, me).wait_send()
-        red(target, me).wait_send()
+        red(lax.rem(me + k, n), me).wait_send()
+        return c
+
+    def drain_chunks(q, c):
+        a2a(q).wait_send()
         return c
 
     lax.fori_loop(1, n, drain, 0)
+    each(0, n, drain_chunks)
+
+
+def finish(*refs):
+    sem = refs[12]
+    steps = []
+    for k in range(4):
+        length = refs[k].shape[0]
+        part = length // 4 if k == 2 else length
+        for lo in range(0, length, part):
+            at = pl.ds(lo, part)
+            m = len(steps)
+            steps.append((
+                pltpu.make_async_copy(refs[k].at[at], refs[8 + k].at[at], sem.at[0, m]),
+                pltpu.make_async_copy(refs[8 + k].at[at], refs[4 + k].at[at], sem.at[1, m]),
+            ))
+    for fetch, _ in steps:
+        fetch.start()
+    for fetch, write in steps:
+        fetch.wait()
+        write.start()
+    for _, write in steps:
+        write.wait()
 
 
 def shards(
@@ -494,16 +569,23 @@
     pairs = rows // 2
     field = jax.ShapeDtypeStruct(displacement.shape, F32)
     vmem = pl.BlockSpec(memory_space=pltpu.VMEM)
-    hbm = pl.BlockSpec(memory_space=pl.ANY)
+    hbm = pl.BlockSpec(memory_space=pltpu.HBM)
     nodes = 8 * (rows + 1)
     dma = pltpu.SemaphoreType.DMA
     out = pl.pallas_call(
         functools.partial(kernel, npx, npy, cap),
         out_shape=(field, field, jax.ShapeDtypeStruct((nh * rows, cols), F32), field),
-        in_specs=[vmem, vmem, vmem, vmem, hbm, hbm, hbm, vmem, vmem, vmem],
+        in_specs=[hbm] * 10,
         out_specs=(vmem, vmem, hbm, vmem),
         scratch_shapes=[
-            pltpu.VMEM((nh, width), F32),
+            pltpu.VMEM(displacement.shape, F32),
+            pltpu.VMEM(displacement.shape, F32),
+            pltpu.VMEM(displacement.shape, F32),
+            pltpu.VMEM(displacement.shape, F32),
+            pltpu.VMEM(stiff_base.shape, F32),
+            pltpu.VMEM(strain_map.shape[::-1], F32),
+            pltpu.VMEM((1, width), jnp.int32),
+            pltpu.VMEM((width + capp, nh), F32),
             pltpu.VMEM((nh * rows, cols), F32),
             pltpu.VMEM((nh * rows, cols), F32),
             pltpu.VMEM((width + capp, nh), F32),
@@ -528,8 +610,7 @@
             pltpu.VMEM((4, 8, 16, cols), F32),
             pltpu.VMEM((8, cols), F32),
             pltpu.VMEM((n, 8, cols), F32),
-            dma((3,)),
-            dma((1,)),
+            dma((11,)),
             dma((n,)),
             dma((n,)),
             dma((4, 8)),
@@ -538,15 +619,24 @@
             dma((n,)),
         ],
         compiler_params=pltpu.CompilerParams(
-            collective_id=0, has_side_effects=True, vmem_limit_bytes=48 << 20
+            collective_id=0, has_side_effects=True, vmem_limit_bytes=63 << 20
         ),
         name="springback",
     )(
         displacement, velocity, load, inv_mass,
         history.reshape(nh * rows, cols), contact_home.reshape(nh * rows, cols),
-        recv_contact.reshape(nh, width), stiff_base, strain_map,
+        jnp.swapaxes(recv_contact.reshape(nh, width), 0, 1), stiff_base, strain_map.T,
         slot_table.reshape(1, width),
     )
+    out = pl.pallas_call(
+        finish,
+        out_shape=tuple(jax.ShapeDtypeStruct(x.shape, F32) for x in out),
+        in_specs=[hbm] * 4,
+        out_specs=(hbm,) * 4,
+        scratch_shapes=[pltpu.VMEM(x.shape, F32) for x in out] + [dma((2, 7))],
+        compiler_params=pltpu.CompilerParams(vmem_limit_bytes=63 << 20),
+        name="finish",
+    )(*out)
     return (out[0], out[1], out[2].reshape(nh, rows, cols), out[3])
 
 

time: 49.7 us -> 46 us (0.926)
  local copies, waits for them, and re-layouts: 6.31 us -> 0 us
  Pallas kernels: 42.4 us -> 45.2 us
    unnamed x22 -> x0, local copies, waits for them, and re-layouts: 6.31 us -> none
    pallas_call x0 -> x1, Pallas kernels: none -> 2.1 us  [shards(): pl.pallas_call(finish, out_shape=tuple((jax.ShapeDtypeStruct(x.shape, F32...]
    pallas_call x1, Pallas kernels: 42.4 us -> 43.1 us  [shards(): pl.pallas_call(functools.partial(kernel, npx, npy, cap), out_shape=(field...]
where the time goes in v2:
time: 46 us; the launch traced here: 45.9 us
  Pallas kernels  45.2 us (98%)
  between operations  0.64 us (1%)
    pallas_call x1, Pallas kernels, shards(): pl.pallas_call(functools.partial(kernel, npx, npy, cap), out_shape=(field...  43.1 us
    pallas_call x1, Pallas kernels, shards(): pl.pallas_call(finish, out_shape=tuple((jax.ShapeDtypeStruct(x.shape, F32...  2.1 us

profile of v2, /device:TPU:0, one launch (start us, length us, event | category | flops | bytes accessed | tf_op | source)
XLA Modules:
  0.0 45.9 jit_solution(6356440556492883740)
XLA Ops:
  0.6 43.1 %springback.1 = (f32[6,16,128]{2,1,0:T(8,128)}, f32[6,16,128]{2,1,0:T(8,128)}, f32[2048,128]{1,0:T(8,128)}, f32[6,16,128]{2,1,0:T(8,128)}) custom-call(f32[6,16,128]{2,1,0:T(8,128)} %disp_hbm.1, f32[6,16,128]{2,1,0:T(8,128)} %vel_hbm.1, f32[6,16,128]{2,1,0:T(8,128)} %load_hbm.1, f32[6,16,128]{2,1,0:T(8,128)} %invm_hbm.1, f32[2048,128]{1,0:T(8,128)} %bitcast.8, ...), custom_call_target="tpu_custom_call" | custom-call | tf_op jit(solution)/shard_map/springback/pallas_call | solution.py:575
  43.8 2.1 %finish.1 = (f32[6,16,128]{2,1,0:T(8,128)}, f32[6,16,128]{2,1,0:T(8,128)}, f32[2048,128]{1,0:T(8,128)}, f32[6,16,128]{2,1,0:T(8,128)}) custom-call(f32[6,16,128]{2,1,0:T(8,128)} %get-tuple-element.12.refs_0_, f32[6,16,128]{2,1,0:T(8,128)} %get-tuple-element.13.refs_1_, f32[2048,128]{1,0:T(8,128)} %get-tuple-element.14.refs_2_, ...), custom_call_target="tpu_custom_call" | custom-call | tf_op jit(solution)/shard_map/finish/pallas_call | solution.py:631
